TPU v7x, 32 devices: a whole 2x2x4 slice. The times are simulated.
32 devices in a mesh: rows: 8 (over z, x), tm: 4 (over y, core).
Axes of the slice: x: 2, y: 2, z: 4, core: 2. Of those that a mesh axis runs over, the one named last changes fastest.
Arguments:
- raw_signal: float32 [256, 64, 128], P('tm', 'rows'), may hold values from -6 to 6
- fir_taps: float32 [61], replicated, may hold values from -0.75 to 0.75
- white_coef: float32 [25, 64, 128], P(None, 'rows'), may hold values from -1.25 to 1.25
- templates: bfloat16 [64, 61, 25], replicated, may hold values from -0.15625 to 0.15625
Outputs:
- whitened: bfloat16 [256, 64, 128], P('tm', 'rows')
- best_score: float32 [256, 64, 128], P('tm', 'rows')
All inputs are finite; a program needn't handle non-finite values.
Results may differ from a plain program's by a relative error of at most 0.0049.
Values may be sent and summed in bfloat16 or wider, within the bound.
A program may use at most 64 MiB of HBM per device.

v0:
```python
import jax
import jax.numpy as jnp
from jax import lax
from jax.sharding import PartitionSpec as P


def shifted_2(array, axis, by):
    size = lax.axis_size(axis)
    pairs = [(i, i + by) for i in range(size) if 0 <= i + by < size]
    return lax.ppermute(array, axis, pairs)


def with_halo(block, sides, width):
    for axis, dim in sides:
        count = lax.axis_size(axis)
        forward = [(i, i + 1) for i in range(count - 1)]
        backward = [(target, source) for source, target in forward]
        low = lax.ppermute(
            lax.slice_in_dim(block, block.shape[dim] - width, None, axis=dim), axis, forward
        )
        high = lax.ppermute(lax.slice_in_dim(block, 0, width, axis=dim), axis, backward)
        block = jnp.concatenate([low, block, high], axis=dim)
    return block


def template_bands(templates, block_len):
    by_spot = jnp.transpose(templates, (0, 2, 1))
    tmpl_len = templates.shape[1]
    shifted = [jnp.pad(by_spot, ((0, 0), (0, 0), (b, block_len - 1 - b))) for b in range(block_len)]
    stacked = jnp.stack(shifted, axis=1)
    spot_major = stacked.reshape(templates.shape[0] * block_len, 25, tmpl_len + block_len - 1)
    return jnp.transpose(spot_major, (0, 2, 1)).reshape(
        templates.shape[0] * block_len, 25 * (tmpl_len + block_len - 1)
    )


def fir_band(fir_taps, num_rows):
    taps_back = fir_taps.shape[0] - 1
    span_len = num_rows + taps_back + 1
    tap_line = jnp.concatenate([fir_taps[::-1], jnp.zeros((num_rows,), jnp.float32)])
    tiled_line = jnp.tile(tap_line, num_rows)[: num_rows * (span_len - 1)]
    return tiled_line.reshape(num_rows, span_len - 1)


def filter_time(extended, fir_taps):
    taps_back = fir_taps.shape[0] - 1
    num_rows = extended.shape[0] - taps_back
    fir_matrix = fir_band(fir_taps, num_rows)
    flattened = extended.reshape(extended.shape[0], -1)
    product = jnp.dot(
        fir_matrix, flattened, precision=lax.Precision.HIGHEST, preferred_element_type=jnp.float32
    )
    return product.reshape(num_rows, extended.shape[1], extended.shape[2]).astype(jnp.bfloat16)


def whiten(rimmed, white_coef):
    row_count = white_coef.shape[1]
    col_count = white_coef.shape[2]
    padded = jnp.pad(rimmed, ((0, 0), (0, 0), (2, 2)))
    summed = jnp.zeros((rimmed.shape[0], row_count, col_count), jnp.float32)
    for row_off in range(5):
        for col_off in range(5):
            summed = summed + white_coef[5 * row_off + col_off] * padded[
                :, row_off : row_off + row_count, col_off : col_off + col_count
            ].astype(jnp.float32)
    return summed.astype(jnp.bfloat16)


def correlate(extended, band_matrix, num_templates, lag_len, step_count):
    block_len = 8
    row_count = extended.shape[1] - 4
    col_count = extended.shape[2]
    padded = jnp.pad(extended, ((0, 0), (0, 0), (2, 2)))
    span_len = padded.shape[0]
    spots = jnp.stack(
        [
            padded[:, row_off : row_off + row_count, col_off : col_off + col_count].reshape(
                span_len, row_count * col_count
            )
            for row_off in range(5)
            for col_off in range(5)
        ],
        axis=1,
    )

    def score_block(i):
        window = lax.dynamic_slice_in_dim(spots, i * block_len, block_len + lag_len, 0)
        flat_window = window.reshape((block_len + lag_len) * 25, row_count * col_count)
        scores = jnp.dot(band_matrix, flat_window, preferred_element_type=jnp.float32)
        return jnp.max(scores.reshape(num_templates, block_len, row_count * col_count), axis=0)

    best_rows = lax.map(score_block, jnp.arange(step_count // block_len, dtype=jnp.int32))
    return best_rows.reshape(step_count, row_count, col_count)


def shards(raw_signal, fir_taps, white_coef, templates):
    step_count = raw_signal.shape[0]
    taps_back = fir_taps.shape[0] - 1
    lag_len = templates.shape[1] - 1
    prev_part = shifted_2(raw_signal[step_count - taps_back :], "tm", 1)
    band_matrix = template_bands(templates, 8)
    filtered = filter_time(jnp.concatenate([prev_part, raw_signal]), fir_taps)
    rimmed = with_halo(filtered, (("rows", 1),), 2)
    whitened = whiten(rimmed, white_coef)
    widened = with_halo(whitened, (("rows", 1),), 2)
    next_part = shifted_2(widened[:lag_len], "tm", -1)
    extended = jnp.concatenate([widened, next_part])
    best_score = correlate(extended, band_matrix, templates.shape[0], lag_len, step_count)
    return (whitened, best_score)


def solution(mesh):
    return jax.shard_map(
        shards,
        mesh=mesh,
        in_specs=(P("tm", "rows", None), P(), P(None, "rows", None), P()),
        out_specs=(P("tm", "rows", None), P("tm", "rows", None)),
        check_vma=False,
    )
```

profile of v0, /device:TPU:1, one launch (start us, length us, event | category | flops | bytes accessed | tf_op | source)
XLA Modules:
  0.0 244.3 jit_solution(7833947067966286846)
XLA Ops:
  1.7 4.5 %collective-permute-start = (f32[60,8,128]{2,1,0:T(8,128)S(1)}, f32[60,8,128]{2,1,0:T(8,128)S(1)}, u32[]{:S(2)}, u32[]{:S(2)}) collective-permute-start(f32[60,8,128]{2,1,0:T(8,128)S(1)} %slice.260), channel_id=1, source_target_pairs={{0,1},{1,2},{2,3},{4,5},{5,6},{6,7},{8,9},{9,10},{10,11},{12,13},{... | collective-permute-start | bytes 737288 | tf_op jit(solution)/shard_map/ppermute | solution.py:10
  27.3 4.1 %collective-permute-start.3 = (bf16[64,2,128]{2,0,1:T(8,128)(2,1)S(1)}, bf16[64,2,128]{2,0,1:T(8,128)(2,1)S(1)}, u32[]{:S(2)}, u32[]{:S(2)}) collective-permute-start(bf16[64,2,128]{2,0,1:T(8,128)(2,1)S(1)} %get-tuple-element.74), channel_id=1, source_target_pairs={{0,4},{4,8},{8,12},{12,16},{16,20},{20,24},{24,28},{1,5},{5,9},{9,... | collective-permute-start | bytes 98312 | tf_op jit(solution)/shard_map/ppermute | solution.py:18
  42.2 4.9 %copy.42 = bf16[64,8,25,68]{3,1,0,2:T(8,128)(2,1)S(1)} copy(bf16[64,8,25,68]{3,0,2,1:T(8,128)(2,1)} %bitcast_dynamic-update-slice_fusion.1) | data formatting | bytes 3481600 | tf_op jit(solution)/shard_map/stack | solution.py:30
  47.1 4.7 %copy.35 = bf16[512,68,25]{0,2,1:T(8,128)(2,1)} copy(bf16[512,68,25]{1,0,2:T(8,128)(2,1)S(1)} %bitcast.188) | data formatting | bytes 3481600 | tf_op jit(solution)/shard_map/transpose | solution.py:32
  112.9 12.0 %copy.36 = bf16[124,25,1024]{2,1,0:T(8,128)(2,1)} copy(bf16[124,25,1024]{0,2,1:T(8,128)(2,1)} %bitcast_dynamic-update-slice_fusion.9) | data formatting | bytes 12697600 | tf_op jit(solution)/shard_map/while | solution.py:92
  124.9 117.7 %while.10 = (s32[]{:T(128)}, f32[8,8,1024]{2,1,0:T(8,128)}, s32[8]{0:T(128)S(1)}, bf16[124,25,1024]{2,1,0:T(8,128)(2,1)}, bf16[512,1700]{1,0:T(8,128)(2,1)}, /*index=5*/s32[]{:T(128)}, s32[1]{0:T(128)}, s32[]{:T(128)}, s32[]{:T(128)}) while((s32[]{:T(128)}, f32[8,8,1024]{2,1,0:T(8,128)}, s32[8]{0:T(128)S(1)}, ...), condition=%wide.region_2.3_spmd, body=%wide.region_0.2_spmd.sunk | while | flops 1783095296 | bytes 19247772 | solution.py:92
  126.1 5.2 %constant_dynamic-slice_fusion.2 = bf16[68,25,1024]{2,1,0:T(8,128)(2,1)} fusion(bf16[124,25,1024]{2,1,0:T(8,128)(2,1)} %get-tuple-element.155, s32[]{:T(128)S(6)} %select_n.4), kind=kLoop, calls=%fused_computation.2.clone.1 | loop fusion | bytes 6963204 | tf_op jit(solution)/shard_map/while/body/eval_jaxpr/dynamic_slice | solution.py:87
  131.3 4.1 %reshape.38 = bf16[1700,1024]{1,0:T(8,128)(2,1)S(1)} reshape(bf16[68,25,1024]{2,1,0:T(8,128)(2,1)} %constant_dynamic-slice_fusion.2) | data formatting | bytes 6963200 | tf_op jit(solution)/shard_map/while/body/eval_jaxpr/reshape | solution.py:88
  140.8 5.2 %constant_dynamic-slice_fusion.2 = bf16[68,25,1024]{2,1,0:T(8,128)(2,1)} fusion(bf16[124,25,1024]{2,1,0:T(8,128)(2,1)} %get-tuple-element.155, s32[]{:T(128)S(6)} %select_n.4), kind=kLoop, calls=%fused_computation.2.clone.1 | loop fusion | bytes 6963204 | tf_op jit(solution)/shard_map/while/body/eval_jaxpr/dynamic_slice | solution.py:87
  146.0 4.1 %reshape.38 = bf16[1700,1024]{1,0:T(8,128)(2,1)S(1)} reshape(bf16[68,25,1024]{2,1,0:T(8,128)(2,1)} %constant_dynamic-slice_fusion.2) | data formatting | bytes 6963200 | tf_op jit(solution)/shard_map/while/body/eval_jaxpr/reshape | solution.py:88
  155.5 5.2 %constant_dynamic-slice_fusion.2 = bf16[68,25,1024]{2,1,0:T(8,128)(2,1)} fusion(bf16[124,25,1024]{2,1,0:T(8,128)(2,1)} %get-tuple-element.155, s32[]{:T(128)S(6)} %select_n.4), kind=kLoop, calls=%fused_computation.2.clone.1 | loop fusion | bytes 6963204 | tf_op jit(solution)/shard_map/while/body/eval_jaxpr/dynamic_slice | solution.py:87
  160.7 4.1 %reshape.38 = bf16[1700,1024]{1,0:T(8,128)(2,1)S(1)} reshape(bf16[68,25,1024]{2,1,0:T(8,128)(2,1)} %constant_dynamic-slice_fusion.2) | data formatting | bytes 6963200 | tf_op jit(solution)/shard_map/while/body/eval_jaxpr/reshape | solution.py:88
  164.8 3.6 %bitcast_reduce_fusion.2 = f32[8,1024]{1,0:T(8,128)S(1)} fusion(bf16[1700,1024]{1,0:T(8,128)(2,1)S(1)} %reshape.38, bf16[512,1700]{1,0:T(8,128)(2,1)} %get-tuple-element.156), kind=kOutput, calls=%fused_computation.clone.1 | convolution fusion | flops 1783095296 | bytes 5255168 | tf_op jit(solution)/shard_map/while/body/eval_jaxpr/dot_general | solution.py:89
  170.2 5.2 %constant_dynamic-slice_fusion.2 = bf16[68,25,1024]{2,1,0:T(8,128)(2,1)} fusion(bf16[124,25,1024]{2,1,0:T(8,128)(2,1)} %get-tuple-element.155, s32[]{:T(128)S(6)} %select_n.4), kind=kLoop, calls=%fused_computation.2.clone.1 | loop fusion | bytes 6963204 | tf_op jit(solution)/shard_map/while/body/eval_jaxpr/dynamic_slice | solution.py:87
  175.4 4.1 %reshape.38 = bf16[1700,1024]{1,0:T(8,128)(2,1)S(1)} reshape(bf16[68,25,1024]{2,1,0:T(8,128)(2,1)} %constant_dynamic-slice_fusion.2) | data formatting | bytes 6963200 | tf_op jit(solution)/shard_map/while/body/eval_jaxpr/reshape | solution.py:88
  184.9 5.2 %constant_dynamic-slice_fusion.2 = bf16[68,25,1024]{2,1,0:T(8,128)(2,1)} fusion(bf16[124,25,1024]{2,1,0:T(8,128)(2,1)} %get-tuple-element.155, s32[]{:T(128)S(6)} %select_n.4), kind=kLoop, calls=%fused_computation.2.clone.1 | loop fusion | bytes 6963204 | tf_op jit(solution)/shard_map/while/body/eval_jaxpr/dynamic_slice | solution.py:87
  190.1 4.1 %reshape.38 = bf16[1700,1024]{1,0:T(8,128)(2,1)S(1)} reshape(bf16[68,25,1024]{2,1,0:T(8,128)(2,1)} %constant_dynamic-slice_fusion.2) | data formatting | bytes 6963200 | tf_op jit(solution)/shard_map/while/body/eval_jaxpr/reshape | solution.py:88
  199.7 5.2 %constant_dynamic-slice_fusion.2 = bf16[68,25,1024]{2,1,0:T(8,128)(2,1)} fusion(bf16[124,25,1024]{2,1,0:T(8,128)(2,1)} %get-tuple-element.155, s32[]{:T(128)S(6)} %select_n.4), kind=kLoop, calls=%fused_computation.2.clone.1 | loop fusion | bytes 6963204 | tf_op jit(solution)/shard_map/while/body/eval_jaxpr/dynamic_slice | solution.py:87
  204.8 4.1 %reshape.38 = bf16[1700,1024]{1,0:T(8,128)(2,1)S(1)} reshape(bf16[68,25,1024]{2,1,0:T(8,128)(2,1)} %constant_dynamic-slice_fusion.2) | data formatting | bytes 6963200 | tf_op jit(solution)/shard_map/while/body/eval_jaxpr/reshape | solution.py:88
  214.4 5.2 %constant_dynamic-slice_fusion.2 = bf16[68,25,1024]{2,1,0:T(8,128)(2,1)} fusion(bf16[124,25,1024]{2,1,0:T(8,128)(2,1)} %get-tuple-element.155, s32[]{:T(128)S(6)} %select_n.4), kind=kLoop, calls=%fused_computation.2.clone.1 | loop fusion | bytes 6963204 | tf_op jit(solution)/shard_map/while/body/eval_jaxpr/dynamic_slice | solution.py:87
  219.5 4.1 %reshape.38 = bf16[1700,1024]{1,0:T(8,128)(2,1)S(1)} reshape(bf16[68,25,1024]{2,1,0:T(8,128)(2,1)} %constant_dynamic-slice_fusion.2) | data formatting | bytes 6963200 | tf_op jit(solution)/shard_map/while/body/eval_jaxpr/reshape | solution.py:88
  223.6 3.6 %bitcast_reduce_fusion.2 = f32[8,1024]{1,0:T(8,128)S(1)} fusion(bf16[1700,1024]{1,0:T(8,128)(2,1)S(1)} %reshape.38, bf16[512,1700]{1,0:T(8,128)(2,1)} %get-tuple-element.156), kind=kOutput, calls=%fused_computation.clone.1 | convolution fusion | flops 1783095296 | bytes 5255168 | tf_op jit(solution)/shard_map/while/body/eval_jaxpr/dot_general | solution.py:89
  229.1 5.2 %constant_dynamic-slice_fusion.2 = bf16[68,25,1024]{2,1,0:T(8,128)(2,1)} fusion(bf16[124,25,1024]{2,1,0:T(8,128)(2,1)} %get-tuple-element.155, s32[]{:T(128)S(6)} %select_n.4), kind=kLoop, calls=%fused_computation.2.clone.1 | loop fusion | bytes 6963204 | tf_op jit(solution)/shard_map/while/body/eval_jaxpr/dynamic_slice | solution.py:87
  234.2 4.1 %reshape.38 = bf16[1700,1024]{1,0:T(8,128)(2,1)S(1)} reshape(bf16[68,25,1024]{2,1,0:T(8,128)(2,1)} %constant_dynamic-slice_fusion.2) | data formatting | bytes 6963200 | tf_op jit(solution)/shard_map/while/body/eval_jaxpr/reshape | solution.py:88
  (123 shorter events, 126.5 us)
Async XLA Ops:
  0.6 22.3 %copy-start = (bf16[64,61,25]{1,0,2:T(8,128)(2,1)S(1)}, bf16[64,61,25]{1,0,2:T(8,128)(2,1)}, u32[]{:S(2)}) copy-start(bf16[64,61,25]{1,0,2:T(8,128)(2,1)} %param.9) | copy-start | bytes 585604
  1.7 14.9 %collective-permute-start = (f32[60,8,128]{2,1,0:T(8,128)S(1)}, f32[60,8,128]{2,1,0:T(8,128)S(1)}, u32[]{:S(2)}, u32[]{:S(2)}) collective-permute-start(f32[60,8,128]{2,1,0:T(8,128)S(1)} %slice.260), channel_id=1, source_target_pairs={{0,1},{1,2},{2,3},{4,5},{5,6},{6,7},{8,9},{9,10},{10,11},{12,13},{... | collective-permute-start | bytes 737288 | tf_op jit(solution)/shard_map/ppermute | solution.py:10
  18.5 5.4 %collective-permute-start.1 = (bf16[64,2,128]{2,0,1:T(8,128)(2,1)S(1)}, bf16[64,2,128]{2,0,1:T(8,128)(2,1)S(1)}, u32[]{:S(2)}, u32[]{:S(2)}) collective-permute-start(bf16[64,2,128]{2,0,1:T(8,128)(2,1)S(1)} %get-tuple-element.76), channel_id=1, source_target_pairs={{0,4},{4,8},{8,12},{12,16},{16,20},{20,24},{24,28},{1,5},{5,9},{9,... | collective-permute-start | bytes 98312 | tf_op jit(solution)/shard_map/ppermute | solution.py:18
  21.6 4.7 %collective-permute-start.2 = (bf16[64,2,128]{2,0,1:T(8,128)(2,1)S(1)}, bf16[64,2,128]{2,0,1:T(8,128)(2,1)S(1)}, u32[]{:S(2)}, u32[]{:S(2)}) collective-permute-start(bf16[64,2,128]{2,0,1:T(8,128)(2,1)S(1)} %get-tuple-element.77), channel_id=1, source_target_pairs={{4,0},{8,4},{12,8},{16,12},{20,16},{24,20},{28,24},{5,1},{9,5},{13... | collective-permute-start | bytes 98312 | tf_op jit(solution)/shard_map/ppermute | solution.py:21
  27.3 6.3 %collective-permute-start.3 = (bf16[64,2,128]{2,0,1:T(8,128)(2,1)S(1)}, bf16[64,2,128]{2,0,1:T(8,128)(2,1)S(1)}, u32[]{:S(2)}, u32[]{:S(2)}) collective-permute-start(bf16[64,2,128]{2,0,1:T(8,128)(2,1)S(1)} %get-tuple-element.74), channel_id=1, source_target_pairs={{0,4},{4,8},{8,12},{12,16},{16,20},{20,24},{24,28},{1,5},{5,9},{9,... | collective-permute-start | bytes 98312 | tf_op jit(solution)/shard_map/ppermute | solution.py:18
  31.4 4.7 %collective-permute-start.4 = (bf16[64,2,128]{2,0,1:T(8,128)(2,1)S(1)}, bf16[64,2,128]{2,0,1:T(8,128)(2,1)S(1)}, u32[]{:S(2)}, u32[]{:S(2)}) collective-permute-start(bf16[64,2,128]{2,0,1:T(8,128)(2,1)S(1)} %get-tuple-element.75), channel_id=1, source_target_pairs={{4,0},{8,4},{12,8},{16,12},{20,16},{24,20},{28,24},{5,1},{9,5},{13... | collective-permute-start | bytes 98312 | tf_op jit(solution)/shard_map/ppermute | solution.py:21
  36.8 20.8 %collective-permute-start.5 = (bf16[60,12,128]{2,0,1:T(8,128)(2,1)}, bf16[60,12,128]{2,0,1:T(8,128)(2,1)}, u32[]{:S(2)}, u32[]{:S(2)}) collective-permute-start(bf16[60,12,128]{2,0,1:T(8,128)(2,1)} %pad_maximum_fusion.2), channel_id=1, source_target_pairs={{1,0},{2,1},{3,2},{5,4},{6,5},{7,6},{9,8},{10,9},{11,10},{13,12},{... | collective-permute-start | bytes 552968 | tf_op jit(solution)/shard_map/ppermute | solution.py:10
  62.4 18.3 %copy-start.3 = (bf16[124,8,128]{2,0,1:T(8,128)(2,1)S(1)}, bf16[124,8,128]{2,0,1:T(8,128)(2,1)}, u32[]{:S(2)}) copy-start(bf16[124,8,128]{2,0,1:T(8,128)(2,1)} %get-tuple-element.63) | copy-start | bytes 761860
  65.8 15.1 %copy-start.2 = (bf16[124,8,128]{2,0,1:T(8,128)(2,1)S(1)}, bf16[124,8,128]{2,0,1:T(8,128)(2,1)}, u32[]{:S(2)}) copy-start(bf16[124,8,128]{2,0,1:T(8,128)(2,1)} %get-tuple-element.64) | copy-start | bytes 761860
  74.0 8.2 %copy-start.1 = (bf16[124,8,128]{2,0,1:T(8,128)(2,1)S(1)}, bf16[124,8,128]{2,0,1:T(8,128)(2,1)}, u32[]{:S(2)}) copy-start(bf16[124,8,128]{2,0,1:T(8,128)(2,1)} %get-tuple-element.66) | copy-start | bytes 761860
where the time goes:
time: 247 us; the launch traced here: 244 us
  local copies, waits for them, and re-layouts  182 us (74%)
  matrix products  29.1 us (12%)
  starting transfers between devices  17.8 us (7%)
  loops' own time  5.39 us (2%)
  waiting for transfers between devices  4.83 us (2%)
  other arithmetic  3.69 us (1%)
    dynamic_slice x8, local copies, waits for them, and re-layouts, score_block(): lax.dynamic_slice_in_dim(spots, i * block_len, block_len + lag_len, 0)  41.3 us
    unnamed x41, local copies, waits for them, and re-layouts  40.9 us
    reshape x8, local copies, waits for them, and re-layouts, score_block(): window.reshape((block_len + lag_len) * 25, row_count * col_count)  32.8 us
    dot_general x8, matrix products, score_block(): jnp.dot(band_matrix, flat_window, preferred_element_type=jnp.float32)  28.5 us
    slice x27, local copies, waits for them, and re-layouts, correlate(): padded[:, row_off:row_off + row_count, col_off:col_off + col_count]  25.5 us
    while x2, local copies, waits for them, and re-layouts, correlate(): lax.map(score_block, jnp.arange(step_count // block_len, dtype=jnp.int32))  14.5 us
    ppermute x2, starting transfers between devices, shifted_2(): return lax.ppermute(array, axis, pairs)  8.03 us
    ppermute x2, starting transfers between devices, with_halo(): lax.ppermute(lax.slice_in_dim(block, block.shape[dim] - width, None, axis...  7.19 us
  transfers between devices with their start and end apart: 6, of which 2 were waited for; matrix products, arithmetic and copies ran while one was open for 12% of the time, Pallas kernels for 0%

commit v1 on v0

v1 whole, which is shorter than its diff:
```python
import jax
import jax.numpy as jnp
from jax import lax
from jax.experimental import pallas as pl
from jax.experimental.pallas import tpu as pltpu
from jax.sharding import PartitionSpec as P

BLOCK = 4


def shifted_2(array, axis, by):
    size = lax.axis_size(axis)
    pairs = [(i, i + by) for i in range(size) if 0 <= i + by < size]
    return lax.ppermute(array, axis, pairs)


def with_halo(block, axis, dim, width):
    low = shifted_2(
        lax.slice_in_dim(block, block.shape[dim] - width, None, axis=dim), axis, 1
    )
    high = shifted_2(lax.slice_in_dim(block, 0, width, axis=dim), axis, -1)
    return jnp.concatenate([low, block, high], axis=dim)


def fir_band(fir_taps, num_rows):
    taps_back = fir_taps.shape[0] - 1
    span_len = num_rows + taps_back + 1
    tap_line = jnp.concatenate([fir_taps[::-1], jnp.zeros((num_rows,), jnp.float32)])
    tiled_line = jnp.tile(tap_line, num_rows)[: num_rows * (span_len - 1)]
    return tiled_line.reshape(num_rows, span_len - 1)


def filter_time(extended, fir_taps):
    taps_back = fir_taps.shape[0] - 1
    num_rows = extended.shape[0] - taps_back
    fir_matrix = fir_band(fir_taps, num_rows)
    flattened = extended.reshape(extended.shape[0], -1)
    product = jnp.dot(
        fir_matrix, flattened, precision=lax.Precision.HIGHEST, preferred_element_type=jnp.float32
    )
    return product.reshape(num_rows, extended.shape[1], extended.shape[2]).astype(jnp.bfloat16)


def whiten(rimmed, white_coef):
    row_count = white_coef.shape[1]
    col_count = white_coef.shape[2]
    padded = jnp.pad(rimmed, ((0, 0), (0, 0), (2, 2)))
    summed = jnp.zeros((rimmed.shape[0], row_count, col_count), jnp.float32)
    for row_off in range(5):
        for col_off in range(5):
            summed = summed + white_coef[5 * row_off + col_off] * padded[
                :, row_off : row_off + row_count, col_off : col_off + col_count
            ].astype(jnp.float32)
    return summed.astype(jnp.bfloat16)


def build_band(tmpl_ref, band_ref):
    spots, count, slot = tmpl_ref.shape
    flat = jnp.concatenate(
        [tmpl_ref[s].astype(jnp.float32) for s in range(spots)]
        + [jnp.zeros((count, slot), jnp.float32)] * (spots % 2),
        axis=1,
    )
    for b in range(BLOCK):
        moved = flat if b == 0 else pltpu.roll(flat, b, 1)
        band_ref[b * count : (b + 1) * count, :] = moved.astype(jnp.bfloat16)


def build_copies(row, block, copies_ref):
    span, cols = block.shape
    lane = lax.broadcasted_iota(jnp.int32, (span, cols), 1)
    for b in range(5):
        by = 2 - b
        moved = block if by == 0 else pltpu.roll(block, by % cols, 1)
        if by > 0:
            moved = jnp.where(lane >= by, moved, 0.0)
        elif by < 0:
            moved = jnp.where(lane < cols + by, moved, 0.0)
        for phase in range(4):
            late = moved if phase == 0 else pltpu.roll(moved, span - 4 * phase, 0)
            copies_ref[b, phase, row] = late.astype(jnp.bfloat16)


def correlate_block(j, copies_ref, band_ref, best_ref, slot):
    count = band_ref.shape[0] // BLOCK
    rows = best_ref.shape[1]
    cols = best_ref.shape[2]
    depth = 25 * slot
    phase = lax.rem(j, 4)
    base = pl.multiple_of((j // 4) * 16, 16)
    band = band_ref[:, :depth]
    for r in range(0, rows, 2):
        patch = jnp.concatenate(
            [
                jnp.concatenate(
                    [copies_ref[b, phase, r + e + a, pl.ds(base, slot), :] for e in range(2)], axis=1
                )
                for a in range(5)
                for b in range(5)
            ],
            axis=0,
        )
        scores = jnp.dot(band, patch, preferred_element_type=jnp.float32)
        for b in range(BLOCK):
            top = jnp.max(scores[b * count : (b + 1) * count], axis=0, keepdims=True)
            for e in range(2):
                best_ref[BLOCK * j + b, r + e : r + e + 1, :] = top[:, e * cols : (e + 1) * cols]


def correlate_kernel(ext_ref, tmpl_ref, best_ref, copies_ref, band_ref):
    slot = tmpl_ref.shape[2]
    build_band(tmpl_ref, band_ref)

    def copies(row, carry):
        build_copies(row, ext_ref[row].astype(jnp.float32), copies_ref)
        return carry

    lax.fori_loop(0, ext_ref.shape[0], copies, 0)

    def step(j, carry):
        correlate_block(j, copies_ref, band_ref, best_ref, slot)
        return carry

    lax.fori_loop(0, best_ref.shape[0] // BLOCK, step, 0)


def correlate(extended, templates, step_count):
    span, rows, cols = extended.shape
    count, tlen, spots = templates.shape
    slot = tlen + BLOCK - 1
    padded_span = -(-span // 16) * 16
    ext = jnp.pad(jnp.transpose(extended, (1, 0, 2)), ((0, 0), (0, padded_span - span), (0, 0)))
    tmpl = jnp.pad(jnp.transpose(templates, (2, 0, 1)), ((0, 0), (0, 0), (0, slot - tlen)))
    return pl.pallas_call(
        correlate_kernel,
        out_shape=jax.ShapeDtypeStruct((step_count, rows - 4, cols), jnp.float32),
        in_specs=[pl.BlockSpec(memory_space=pltpu.VMEM)] * 2,
        out_specs=pl.BlockSpec(memory_space=pltpu.VMEM),
        scratch_shapes=[
            pltpu.VMEM((5, 4, rows, padded_span, cols), jnp.bfloat16),
            pltpu.VMEM((BLOCK * count, (spots + spots % 2) * slot), jnp.bfloat16),
        ],
        compiler_params=pltpu.CompilerParams(vmem_limit_bytes=40 * 2**20),
    )(ext, tmpl)


def shards(raw_signal, fir_taps, white_coef, templates):
    step_count = raw_signal.shape[0]
    taps_back = fir_taps.shape[0] - 1
    lag_len = templates.shape[1] - 1
    prev_part = shifted_2(raw_signal[step_count - taps_back :], "tm", 1)
    filtered = filter_time(jnp.concatenate([prev_part, raw_signal]), fir_taps)
    rimmed = with_halo(filtered, "rows", 1, 2)
    whitened = whiten(rimmed, white_coef)
    widened = with_halo(whitened, "rows", 1, 2)
    next_part = shifted_2(widened[:lag_len], "tm", -1)
    extended = jnp.concatenate([widened, next_part])
    best_score = correlate(extended, templates, step_count)
    return (whitened, best_score)


def solution(mesh):
    return jax.shard_map(
        shards,
        mesh=mesh,
        in_specs=(P("tm", "rows", None), P(), P(None, "rows", None), P()),
        out_specs=(P("tm", "rows", None), P("tm", "rows", None)),
        check_vma=False,
    )
```

time: 247 us -> 59.8 us (0.24); the launches traced: 244 us -> 59.6 us
  local copies, waits for them, and re-layouts: 182 us -> 2.52 us
  matrix products: 29.1 us -> 0.65 us
  Pallas kernels: 0 us -> 20.7 us
  waiting for transfers between devices: 4.83 us -> 17.2 us
  loops' own time: 5.39 us -> 0 us
  other arithmetic: 3.69 us -> 1.14 us
    dynamic_slice x16 -> x0, local copies, waits for them, and re-layouts: 46 us -> none  [the longest x8 41.3 us: score_block(): lax.dynamic_slice_in_dim(spots, i * block_len, block_len + lag_len, 0)]
    unnamed x41 -> x9, local copies, waits for them, and re-layouts: 40.9 us -> 0.77 us
    reshape x9 -> x0, local copies, waits for them, and re-layouts: 35.4 us -> none  [the longest x8 32.8 us: score_block(): window.reshape((block_len + lag_len) * 25, row_count * col_count)]
    dot_general x8 -> x0, matrix products: 28.5 us -> none  [score_block(): jnp.dot(band_matrix, flat_window, preferred_element_type=jnp.float32)]
    slice x27 -> x0, local copies, waits for them, and re-layouts: 25.5 us -> none  [correlate(): padded[:, row_off:row_off + row_count, col_off:col_off + col_count]]
    pallas_call x0 -> x1, Pallas kernels: none -> 20.7 us  [correlate(): pl.pallas_call(correlate_kernel, out_shape=jax.ShapeDtypeStruct((step_cou...]
    ppermute x2 -> x6, waiting for transfers between devices: 0.01 us -> 17.2 us  [shifted_2(): return lax.ppermute(array, axis, pairs)]
    while x2 -> x0, local copies, waits for them, and re-layouts: 14.5 us -> none  [correlate(): lax.map(score_block, jnp.arange(step_count // block_len, dtype=jnp.int32))]
  transfers between devices with their start and end apart: 6 -> 6, of which waited for: 2 -> 4; matrix products, arithmetic and copies ran while one was open for 12% -> 2% of each run, Pallas kernels for 0% -> 0%
where the time goes in v1:
time: 59.8 us; the launch traced here: 59.6 us
  Pallas kernels  20.7 us (35%)
  waiting for transfers between devices  17.2 us (29%)
  starting transfers between devices  16.5 us (28%)
  local copies, waits for them, and re-layouts  2.52 us (4%)
  other arithmetic  1.14 us (2%)
  between operations  0.86 us (1%)
  matrix products  0.65 us (1%)
    pallas_call x1, Pallas kernels, correlate(): pl.pallas_call(correlate_kernel, out_shape=jax.ShapeDtypeStruct((step_cou...  20.7 us
    ppermute x6, waiting for transfers between devices, shifted_2(): return lax.ppermute(array, axis, pairs)  17.2 us
    ppermute x6, starting transfers between devices, shifted_2(): return lax.ppermute(array, axis, pairs)  16.5 us
  transfers between devices with their start and end apart: 6, of which 4 were waited for; matrix products, arithmetic and copies ran while one was open for 2% of the time, Pallas kernels for 0%

profile of v1, /device:TPU:1, one launch (start us, length us, event | category | flops | bytes accessed | tf_op | source)
XLA Modules:
  0.0 59.6 jit_solution(2051760202691815939)
XLA Ops:
  0.6 1.0 %slice.180 = f32[60,8,128]{2,1,0:T(8,128)S(1)} slice(f32[64,8,128]{2,1,0:T(8,128)} %param.4), slice={[4:64], [0:8], [0:128]} | slice | bytes 491520 | tf_op jit(solution)/shard_map/slice | solution.py:151
  1.7 0.0 copy-start
  1.7 4.7 %collective-permute-start = (f32[60,8,128]{2,1,0:T(8,128)S(1)}, f32[60,8,128]{2,1,0:T(8,128)S(1)}, u32[]{:S(2)}, u32[]{:S(2)}) collective-permute-start(f32[60,8,128]{2,1,0:T(8,128)S(1)} %slice.180), channel_id=1, source_target_pairs={{0,1},{1,2},{2,3},{4,5},{5,6},{6,7},{8,9},{9,10},{10,11},{12,13},{... | collective-permute-start | bytes 737288 | tf_op jit(solution)/shard_map/ppermute | solution.py:14
  6.3 0.1 rev.3
  6.5 0.1 tile.10
  6.6 0.1 reshape.15
  6.7 2.7 %collective-permute-done = f32[60,8,128]{2,1,0:T(8,128)S(1)} collective-permute-done((f32[60,8,128]{2,1,0:T(8,128)S(1)}, f32[60,8,128]{2,1,0:T(8,128)S(1)}, u32[]{:S(2)}, u32[]{:S(2)}) %collective-permute-start) | collective-permute-done | bytes 245792 | tf_op jit(solution)/shard_map/ppermute | solution.py:14
  9.5 0.2 copy.8
  9.7 0.6 %convolution_convert_fusion = bf16[64,8,128]{2,0,1:T(8,128)(2,1)S(1)} fusion(f32[64,124,1]{1,0,2:T(8,128)S(1)} %reshape.15, f32[124,8,128]{0,2,1:T(8,128)S(1)} %copy.8), kind=kOutput, calls=%fused_computation.2 | convolution fusion | flops 97583104 | bytes 670720 | tf_op jit(solution)/shard_map/dot_general | solution.py:38
  10.4 3.1 %collective-permute-start.1 = (bf16[64,2,128]{2,0,1:T(8,128)(2,1)S(1)}, bf16[64,2,128]{2,0,1:T(8,128)(2,1)S(1)}, u32[]{:S(2)}, u32[]{:S(2)}) collective-permute-start(bf16[64,2,128]{2,0,1:T(8,128)(2,1)S(1)} %get-tuple-element.6), channel_id=1, source_target_pairs={{0,4},{4,8},{8,12},{12,16},{16,20},{20,24},{24,28},{1,5},{5,9},{9,... | collective-permute-start | bytes 98312 | tf_op jit(solution)/shard_map/ppermute | solution.py:14
  13.5 1.3 %collective-permute-start.2 = (bf16[64,2,128]{2,0,1:T(8,128)(2,1)S(1)}, bf16[64,2,128]{2,0,1:T(8,128)(2,1)S(1)}, u32[]{:S(2)}, u32[]{:S(2)}) collective-permute-start(bf16[64,2,128]{2,0,1:T(8,128)(2,1)S(1)} %get-tuple-element.7), channel_id=1, source_target_pairs={{4,0},{8,4},{12,8},{16,12},{20,16},{24,20},{28,24},{5,1},{9,5},{13... | collective-permute-start | bytes 98312 | tf_op jit(solution)/shard_map/ppermute | solution.py:14
  14.9 0.0 collective-permute-done.1
  14.9 3.3 %collective-permute-done.2 = bf16[64,2,128]{2,0,1:T(8,128)(2,1)S(1)} collective-permute-done((bf16[64,2,128]{2,0,1:T(8,128)(2,1)S(1)}, bf16[64,2,128]{2,0,1:T(8,128)(2,1)S(1)}, u32[]{:S(2)}, u32[]{:S(2)}) %collective-permute-start.2) | collective-permute-done | bytes 32800 | tf_op jit(solution)/shard_map/ppermute | solution.py:14
  18.2 0.2 fusion.6
  18.4 0.9 %add_convert_fusion = bf16[64,8,128]{2,0,1:T(8,128)(2,1)S(1)} fusion(bf16[64,8,128]{2,0,1:T(8,128)(2,1)S(1)} %convolution_convert_fusion, bf16[64,2,128]{2,0,1:T(8,128)(2,1)S(1)} %collective-permute-done.2, bf16[64,2,128]{2,0,1:T(8,128)(2,1)S(1)} %collective-permute-done.1, bf16[64,12,132]{2,0,1:T(8,128)(2,1)S(1)} %fusion.6, ...), kind=kLoop, calls=%fused_computation.12 | loop fusion | flops 5177344 | bytes 3051520 | tf_op jit(solution)/shard_map/convert_element_type | solution.py:54
  19.3 0.0 copy-start.1
  19.3 4.2 %collective-permute-start.3 = (bf16[64,2,128]{2,0,1:T(8,128)(2,1)S(1)}, bf16[64,2,128]{2,0,1:T(8,128)(2,1)S(1)}, u32[]{:S(2)}, u32[]{:S(2)}) collective-permute-start(bf16[64,2,128]{2,0,1:T(8,128)(2,1)S(1)} %get-tuple-element.4), channel_id=1, source_target_pairs={{0,4},{4,8},{8,12},{12,16},{16,20},{20,24},{24,28},{1,5},{5,9},{9,... | collective-permute-start | bytes 98312 | tf_op jit(solution)/shard_map/ppermute | solution.py:14
  23.5 1.3 %collective-permute-start.4 = (bf16[64,2,128]{2,0,1:T(8,128)(2,1)S(1)}, bf16[64,2,128]{2,0,1:T(8,128)(2,1)S(1)}, u32[]{:S(2)}, u32[]{:S(2)}) collective-permute-start(bf16[64,2,128]{2,0,1:T(8,128)(2,1)S(1)} %get-tuple-element.5), channel_id=1, source_target_pairs={{4,0},{8,4},{12,8},{16,12},{20,16},{24,20},{28,24},{5,1},{9,5},{13... | collective-permute-start | bytes 98312 | tf_op jit(solution)/shard_map/ppermute | solution.py:14
  24.8 3.3 %collective-permute-done.4 = bf16[64,2,128]{2,0,1:T(8,128)(2,1)S(1)} collective-permute-done((bf16[64,2,128]{2,0,1:T(8,128)(2,1)S(1)}, bf16[64,2,128]{2,0,1:T(8,128)(2,1)S(1)}, u32[]{:S(2)}, u32[]{:S(2)}) %collective-permute-start.4) | collective-permute-done | bytes 32800 | tf_op jit(solution)/shard_map/ppermute | solution.py:14
  28.2 1.9 %collective-permute-start.5 = (bf16[60,12,128]{2,0,1:T(8,128)(2,1)S(1)}, bf16[60,12,128]{2,0,1:T(8,128)(2,1)S(1)}, u32[]{:S(2)}, u32[]{:S(2)}) collective-permute-start(bf16[60,12,128]{2,0,1:T(8,128)(2,1)S(1)} %pad_maximum_fusion.1), channel_id=1, source_target_pairs={{1,0},{2,1},{3,2},{5,4},{6,5},{7,6},{9,8},{10,9},{11,10},{13,12},{... | collective-permute-start | bytes 552968 | tf_op jit(solution)/shard_map/ppermute | solution.py:14
  30.1 0.1 pad.15.tmpl_ref
  30.2 0.7 %copy.7 = bf16[64,8,128]{2,1,0:T(8,128)(2,1)} copy(bf16[64,8,128]{2,0,1:T(8,128)(2,1)S(1)} %add_convert_fusion) | data formatting | bytes 262144
  31.0 7.8 %collective-permute-done.5 = bf16[60,12,128]{2,0,1:T(8,128)(2,1)S(1)} collective-permute-done((bf16[60,12,128]{2,0,1:T(8,128)(2,1)S(1)}, bf16[60,12,128]{2,0,1:T(8,128)(2,1)S(1)}, u32[]{:S(2)}, u32[]{:S(2)}) %collective-permute-start.5) | collective-permute-done | bytes 184352 | tf_op jit(solution)/shard_map/ppermute | solution.py:14
  38.9 20.7 %shard_map.59 = f32[64,8,128]{2,1,0:T(8,128)} custom-call(bf16[12,128,128]{2,1,0:T(8,128)(2,1)S(1)} %pad.14.ext_ref, bf16[25,64,64]{2,1,0:T(8,128)(2,1)S(1)} %pad.15.tmpl_ref), custom_call_target="tpu_custom_call" | custom-call | tf_op jit(solution)/shard_map/pallas_call | solution.py:134
  (17 shorter events, 0.2 us)
Async XLA Ops:
  0.6 5.7 %copy-start.3 = (f32[61]{0:T(128)S(1)}, f32[61]{0:T(128)}, u32[]{:S(2)}) copy-start(f32[61]{0:T(128)} %param.5) | copy-start | bytes 736
  0.6 6.1 %copy-start.2 = (f32[25,8,128]{2,1,0:T(8,128)S(1)}, f32[25,8,128]{2,1,0:T(8,128)}, u32[]{:S(2)}) copy-start(f32[25,8,128]{2,1,0:T(8,128)} %param.6) | copy-start | bytes 307204
  1.7 7.8 %copy-start = (f32[64,8,128]{2,1,0:T(8,128)S(1)}, f32[64,8,128]{2,1,0:T(8,128)}, u32[]{:S(2)}) copy-start(f32[64,8,128]{2,1,0:T(8,128)} %param.4) | copy-start | bytes 786436
  1.7 7.8 %collective-permute-start = (f32[60,8,128]{2,1,0:T(8,128)S(1)}, f32[60,8,128]{2,1,0:T(8,128)S(1)}, u32[]{:S(2)}, u32[]{:S(2)}) collective-permute-start(f32[60,8,128]{2,1,0:T(8,128)S(1)} %slice.180), channel_id=1, source_target_pairs={{0,1},{1,2},{2,3},{4,5},{5,6},{6,7},{8,9},{9,10},{10,11},{12,13},{... | collective-permute-start | bytes 737288 | tf_op jit(solution)/shard_map/ppermute | solution.py:14
  10.4 4.4 %collective-permute-start.1 = (bf16[64,2,128]{2,0,1:T(8,128)(2,1)S(1)}, bf16[64,2,128]{2,0,1:T(8,128)(2,1)S(1)}, u32[]{:S(2)}, u32[]{:S(2)}) collective-permute-start(bf16[64,2,128]{2,0,1:T(8,128)(2,1)S(1)} %get-tuple-element.6), channel_id=1, source_target_pairs={{0,4},{4,8},{8,12},{12,16},{16,20},{20,24},{24,28},{1,5},{5,9},{9,... | collective-permute-start | bytes 98312 | tf_op jit(solution)/shard_map/ppermute | solution.py:14
  13.5 4.7 %collective-permute-start.2 = (bf16[64,2,128]{2,0,1:T(8,128)(2,1)S(1)}, bf16[64,2,128]{2,0,1:T(8,128)(2,1)S(1)}, u32[]{:S(2)}, u32[]{:S(2)}) collective-permute-start(bf16[64,2,128]{2,0,1:T(8,128)(2,1)S(1)} %get-tuple-element.7), channel_id=1, source_target_pairs={{4,0},{8,4},{12,8},{16,12},{20,16},{24,20},{28,24},{5,1},{9,5},{13... | collective-permute-start | bytes 98312 | tf_op jit(solution)/shard_map/ppermute | solution.py:14
  19.3 10.8 %copy-start.1 = (bf16[64,61,25]{1,0,2:T(8,128)(2,1)S(1)}, bf16[64,61,25]{1,0,2:T(8,128)(2,1)}, u32[]{:S(2)}) copy-start(bf16[64,61,25]{1,0,2:T(8,128)(2,1)} %param.7) | copy-start | bytes 585604
  19.3 5.5 %collective-permute-start.3 = (bf16[64,2,128]{2,0,1:T(8,128)(2,1)S(1)}, bf16[64,2,128]{2,0,1:T(8,128)(2,1)S(1)}, u32[]{:S(2)}, u32[]{:S(2)}) collective-permute-start(bf16[64,2,128]{2,0,1:T(8,128)(2,1)S(1)} %get-tuple-element.4), channel_id=1, source_target_pairs={{0,4},{4,8},{8,12},{12,16},{16,20},{20,24},{24,28},{1,5},{5,9},{9,... | collective-permute-start | bytes 98312 | tf_op jit(solution)/shard_map/ppermute | solution.py:14
  23.5 4.7 %collective-permute-start.4 = (bf16[64,2,128]{2,0,1:T(8,128)(2,1)S(1)}, bf16[64,2,128]{2,0,1:T(8,128)(2,1)S(1)}, u32[]{:S(2)}, u32[]{:S(2)}) collective-permute-start(bf16[64,2,128]{2,0,1:T(8,128)(2,1)S(1)} %get-tuple-element.5), channel_id=1, source_target_pairs={{4,0},{8,4},{12,8},{16,12},{20,16},{24,20},{28,24},{5,1},{9,5},{13... | collective-permute-start | bytes 98312 | tf_op jit(solution)/shard_map/ppermute | solution.py:14
  28.2 10.6 %collective-permute-start.5 = (bf16[60,12,128]{2,0,1:T(8,128)(2,1)S(1)}, bf16[60,12,128]{2,0,1:T(8,128)(2,1)S(1)}, u32[]{:S(2)}, u32[]{:S(2)}) collective-permute-start(bf16[60,12,128]{2,0,1:T(8,128)(2,1)S(1)} %pad_maximum_fusion.1), channel_id=1, source_target_pairs={{1,0},{2,1},{3,2},{5,4},{6,5},{7,6},{9,8},{10,9},{11,10},{13,12},{... | collective-permute-start | bytes 552968 | tf_op jit(solution)/shard_map/ppermute | solution.py:14

commit v2 on v1

v2 whole, which is shorter than its diff:
```python
import functools

import jax
import jax.numpy as jnp
from jax import lax
from jax.experimental import pallas as pl
from jax.experimental.pallas import tpu as pltpu
from jax.sharding import PartitionSpec as P

BLOCK = 4
EDGE = 2


def build_band(tmpl_ref, band_ref):
    spots, count, slot = tmpl_ref.shape
    flat = jnp.concatenate(
        [tmpl_ref[s].astype(jnp.float32) for s in range(spots)]
        + [jnp.zeros((count, slot), jnp.float32)] * (spots % 2),
        axis=1,
    )
    for b in range(BLOCK):
        moved = flat if b == 0 else pltpu.roll(flat, b, 1)
        band_ref[b * count : (b + 1) * count, :] = moved.astype(jnp.bfloat16)


def build_copies(row, block, copies_ref):
    span, cols = block.shape
    lane = lax.broadcasted_iota(jnp.int32, (span, cols), 1)
    for b in range(5):
        by = 2 - b
        moved = block if by == 0 else pltpu.roll(block, by % cols, 1)
        if by > 0:
            moved = jnp.where(lane >= by, moved, 0.0)
        elif by < 0:
            moved = jnp.where(lane < cols + by, moved, 0.0)
        for phase in range(4):
            late = moved if phase == 0 else pltpu.roll(moved, span - 4 * phase, 0)
            copies_ref[b, phase, row] = late.astype(jnp.bfloat16)


def correlate_block(j, copies_ref, band_ref, best_ref, slot):
    count = band_ref.shape[0] // BLOCK
    rows = best_ref.shape[1]
    cols = best_ref.shape[2]
    depth = 25 * slot
    phase = lax.rem(j, 4)
    base = pl.multiple_of((j // 4) * 16, 16)
    band = band_ref[:, :depth]
    for r in range(0, rows, 2):
        patch = jnp.concatenate(
            [
                jnp.concatenate(
                    [copies_ref[b, phase, r + e + a, pl.ds(base, slot), :] for e in range(2)], axis=1
                )
                for a in range(5)
                for b in range(5)
            ],
            axis=0,
        )
        scores = jnp.dot(band, patch, preferred_element_type=jnp.float32)
        for b in range(BLOCK):
            top = jnp.max(scores[b * count : (b + 1) * count], axis=0, keepdims=True)
            for e in range(2):
                best_ref[BLOCK * j + b, r + e : r + e + 1, :] = top[:, e * cols : (e + 1) * cols]


def filter_rows(line_ref, ext_ref, filt_ref):
    span, rows, cols = ext_ref.shape
    steps = filt_ref.shape[1]
    line = jnp.broadcast_to(line_ref[...], (steps, span))
    toeplitz = pltpu.roll(line, 0, 1, stride=1, stride_axis=0)
    flat = jnp.concatenate([ext_ref[:, r, :] for r in range(rows)], axis=1)
    product = jnp.dot(
        toeplitz, flat, precision=lax.Precision.HIGHEST, preferred_element_type=jnp.float32
    )
    for r in range(rows):
        filt_ref[2 * EDGE + r] = product[:, r * cols : (r + 1) * cols].astype(jnp.bfloat16)


def shift_columns(block, by):
    cols = block.shape[1]
    if by == 0:
        return block
    lane = lax.broadcasted_iota(jnp.int32, block.shape, 1)
    moved = pltpu.roll(block, by % cols, 1)
    keep = lane >= by if by > 0 else lane < cols + by
    return jnp.where(keep, moved, 0.0)


def whiten_rows(filt_ref, moved_ref, coef_ref, white_ref, turned_ref):
    def move(row, carry):
        block = filt_ref[row].astype(jnp.float32)
        for b in range(5):
            moved_ref[b, row] = shift_columns(block, 2 - b)
        return carry

    lax.fori_loop(0, filt_ref.shape[0], move, 0)

    def one(row):
        total = None
        for a in range(5):
            for b in range(5):
                spot = 5 * a + b
                term = coef_ref[row, spot : spot + 1, :] * moved_ref[b, row + a]
                total = term if total is None else total + term
        white_ref[0, row] = total.astype(jnp.bfloat16)
        return total

    for row in range(coef_ref.shape[0]):
        total = one(row)
        if EDGE <= row < coef_ref.shape[0] - EDGE:
            turned_ref[:, row - EDGE, :] = total


def fused_kernel(
    row_parts, time_parts, taps_back,
    raw_ref, line_ref, coef_in_ref, tmpl_ref, white_out_ref, best_ref,
    ext_ref, coef_ref, filt_ref, moved_ref, white_ref, turned_ref, copies_ref, band_ref,
    send_sem, recv_sem,
):
    steps, rows, cols = raw_ref.shape
    slot = tmpl_ref.shape[2]
    spots = coef_in_ref.shape[0]
    row_at = lax.axis_index("rows")
    time_at = lax.axis_index("tm")
    has_low = row_at > 0
    has_high = row_at < row_parts - 1
    has_prev = time_at > 0
    has_next = time_at < time_parts - 1
    low = {"rows": row_at - 1}
    high = {"rows": row_at + 1}
    prev = {"tm": time_at - 1}
    later = {"tm": time_at + 1}

    ext_ref[0:steps] = jnp.zeros((steps, rows, cols), jnp.float32)
    coef_ref[...] = jnp.zeros(coef_ref.shape, jnp.float32)
    filt_ref[0 : 2 * EDGE] = jnp.zeros((2 * EDGE, steps, cols), jnp.bfloat16)
    filt_ref[2 * EDGE + rows :] = jnp.zeros((2 * EDGE, steps, cols), jnp.bfloat16)
    white_ref[1] = jnp.zeros(white_ref.shape[1:], jnp.bfloat16)
    for r in range(rows):
        coef_ref[EDGE + r, 0:spots, :] = coef_in_ref[:, r, :]

    barrier = pltpu.get_barrier_semaphore()
    sides = ((has_low, low), (has_high, high), (has_prev, prev), (has_next, later))
    for there, where in sides:
        @pl.when(there)
        def _():
            pl.semaphore_signal(
                barrier, inc=1, device_id=where, device_id_type=pl.DeviceIdType.MESH
            )
    peers = sum(
        (at + parts - 1) // parts + (2 * parts - 2 - at) // parts
        for at, parts in ((row_at, row_parts), (time_at, time_parts))
    )
    pl.semaphore_wait(barrier, peers)

    def remote(index, source, target, where):
        return pltpu.make_async_remote_copy(
            src_ref=source,
            dst_ref=target,
            send_sem=send_sem.at[index],
            recv_sem=recv_sem.at[index],
            device_id=where,
            device_id_type=pl.DeviceIdType.MESH,
        )

    lead = steps - taps_back
    top = 2 * EDGE + rows
    raw_copy = remote(0, raw_ref.at[lead:steps], ext_ref.at[lead:steps], later)
    coef_down = remote(1, coef_ref.at[EDGE : 2 * EDGE], coef_ref.at[EDGE + rows : 2 * EDGE + rows], low)
    coef_up = remote(2, coef_ref.at[rows : EDGE + rows], coef_ref.at[0:EDGE], high)
    filt_down = remote(3, filt_ref.at[2 * EDGE : 4 * EDGE], filt_ref.at[top : top + 2 * EDGE], low)
    filt_up = remote(4, filt_ref.at[rows:top], filt_ref.at[0 : 2 * EDGE], high)
    white_copy = remote(5, white_ref.at[0], white_ref.at[1], prev)

    def start(copy, there):
        @pl.when(there)
        def _():
            copy.start()

    def sent(copy, there):
        @pl.when(there)
        def _():
            copy.wait_send()

    def arrived(copy, there):
        @pl.when(there)
        def _():
            copy.wait_recv()

    start(raw_copy, has_next)
    start(coef_down, has_low)
    start(coef_up, has_high)
    ext_ref[steps:] = raw_ref[...]
    build_band(tmpl_ref, band_ref)
    arrived(raw_copy, has_prev)
    filter_rows(line_ref, ext_ref, filt_ref)
    start(filt_down, has_low)
    start(filt_up, has_high)
    arrived(coef_down, has_high)
    arrived(coef_up, has_low)
    arrived(filt_down, has_high)
    arrived(filt_up, has_low)
    whiten_rows(filt_ref, moved_ref, coef_ref, white_ref, turned_ref)
    start(white_copy, has_prev)
    white_out_ref[...] = turned_ref[...].astype(jnp.bfloat16)
    arrived(white_copy, has_next)

    def copies(row, carry):
        block = jnp.concatenate([white_ref[0, row], white_ref[1, row]], axis=0)
        build_copies(row, block.astype(jnp.float32), copies_ref)
        return carry

    lax.fori_loop(0, rows + 2 * EDGE, copies, 0)

    def step(j, carry):
        correlate_block(j, copies_ref, band_ref, best_ref, slot)
        return carry

    lax.fori_loop(0, steps // BLOCK, step, 0)
    sent(raw_copy, has_next)
    sent(coef_down, has_low)
    sent(coef_up, has_high)
    sent(filt_down, has_low)
    sent(filt_up, has_high)
    sent(white_copy, has_prev)


def shards(raw_signal, fir_taps, white_coef, templates):
    steps, rows, cols = raw_signal.shape
    count, tlen, spots = templates.shape
    taps_back = fir_taps.shape[0] - 1
    lead = steps - taps_back
    slot = tlen + BLOCK - 1
    tmpl = jnp.pad(jnp.transpose(templates, (2, 0, 1)), ((0, 0), (0, 0), (0, slot - tlen)))
    line = jnp.pad(fir_taps[::-1], (lead, 2 * steps - lead - taps_back - 1)).reshape(1, 2 * steps)
    wide = rows + 2 * EDGE
    vmem = pl.BlockSpec(memory_space=pltpu.VMEM)
    kernel = functools.partial(
        fused_kernel, lax.axis_size("rows"), lax.axis_size("tm"), taps_back
    )
    return pl.pallas_call(
        kernel,
        out_shape=(
            jax.ShapeDtypeStruct((steps, rows, cols), jnp.bfloat16),
            jax.ShapeDtypeStruct((steps, rows, cols), jnp.float32),
        ),
        in_specs=[vmem] * 4,
        out_specs=(vmem, vmem),
        scratch_shapes=[
            pltpu.VMEM((2 * steps, rows, cols), jnp.float32),
            pltpu.VMEM((wide, 32, cols), jnp.float32),
            pltpu.VMEM((rows + 4 * EDGE, steps, cols), jnp.bfloat16),
            pltpu.VMEM((5, rows + 4 * EDGE, steps, cols), jnp.float32),
            pltpu.VMEM((2, wide, steps, cols), jnp.bfloat16),
            pltpu.VMEM((steps, rows, cols), jnp.float32),
            pltpu.VMEM((5, 4, wide, 2 * steps, cols), jnp.bfloat16),
            pltpu.VMEM((BLOCK * count, (spots + spots % 2) * slot), jnp.bfloat16),
            pltpu.SemaphoreType.DMA((6,)),
            pltpu.SemaphoreType.DMA((6,)),
        ],
        compiler_params=pltpu.CompilerParams(
            collective_id=0, has_side_effects=True, vmem_limit_bytes=48 * 2**20
        ),
    )(raw_signal, line, white_coef, tmpl)


def solution(mesh):
    return jax.shard_map(
        shards,
        mesh=mesh,
        in_specs=(P("tm", "rows", None), P(), P(None, "rows", None), P()),
        out_specs=(P("tm", "rows", None), P("tm", "rows", None)),
        check_vma=False,
    )
```

time: 59.8 us -> 42.4 us (0.71)
  Pallas kernels: 20.7 us -> 38.2 us
  waiting for transfers between devices: 17.2 us -> 0 us
  starting transfers between devices: 16.5 us -> 0 us
  other arithmetic: 1.14 us -> 0 us
  local copies, waits for them, and re-layouts: 2.52 us -> 3.34 us
  matrix products: 0.65 us -> 0 us
    pallas_call x1, Pallas kernels: 20.7 us -> 38.2 us  [shards(): pl.pallas_call(kernel, out_shape=(jax.ShapeDtypeStruct((steps, rows, cols...]
    ppermute x6 -> x0, waiting for transfers between devices: 17.2 us -> none  [shifted_2(): return lax.ppermute(array, axis, pairs)]
    ppermute x6 -> x0, starting transfers between devices: 16.5 us -> none  [shifted_2(): return lax.ppermute(array, axis, pairs)]
    unnamed x9 -> x8, local copies, waits for them, and re-layouts: 0.77 us -> 2.02 us
    slice x3 -> x0, local copies, waits for them, and re-layouts: 1.01 us -> none  [the longest x1 1 us: shards(): prev_part = shifted_2(raw_signal[step_count - taps_back:], 'tm', 1)]
    pad x2 -> x1, local copies, waits for them, and re-layouts: 0.14 us -> 1.15 us  [shards(): jnp.pad(jnp.transpose(templates, (2, 0, 1)), ((0, 0), (0, 0), (0, slot -...]
    convert_element_type x1 -> x0, other arithmetic: 0.86 us -> none  [whiten(): return summed.astype(jnp.bfloat16)]
    dot_general x1 -> x0, matrix products: 0.65 us -> none  [filter_time(): jnp.dot(fir_matrix, flattened, precision=lax.Precision.HIGHEST, preferred...]
  transfers between devices with their start and end apart: 6 -> 0, of which waited for: 4 -> 0; matrix products, arithmetic and copies ran while one was open for 2% -> 0% of each run, Pallas kernels for 0% -> 0%
where the time goes in v2:
time: 42.4 us; the launch traced here: 42.2 us
  Pallas kernels  38.2 us (90%)
  local copies, waits for them, and re-layouts  3.34 us (8%)
  between operations  0.67 us (2%)
    pallas_call x1, Pallas kernels, shards(): pl.pallas_call(kernel, out_shape=(jax.ShapeDtypeStruct((steps, rows, cols...  38.2 us
    unnamed x8, local copies, waits for them, and re-layouts  2.02 us
    pad x1, local copies, waits for them, and re-layouts, shards(): jnp.pad(jnp.transpose(templates, (2, 0, 1)), ((0, 0), (0, 0), (0, slot -...  1.15 us

profile of v2, /device:TPU:1, one launch (start us, length us, event | category | flops | bytes accessed | tf_op | source)
XLA Modules:
  0.0 42.2 jit_solution(17895444282800897600)
XLA Ops:
  0.6 0.0 copy-start.2
  0.6 0.6 %copy-done.2 = f32[61]{0:T(128)S(1)} copy-done((f32[61]{0:T(128)S(1)}, f32[61]{0:T(128)}, u32[]{:S(2)}) %copy-start.2) | copy-done | bytes 268
  1.3 0.1 rev.3
  1.4 0.1 pad_bitcast_fusion.line_ref
  1.5 0.0 copy-start
  1.5 0.0 copy-start.1
  1.5 1.1 %pad.9.tmpl_ref = bf16[25,64,64]{2,1,0:T(8,128)(2,1)S(1)} pad(bf16[25,64,61]{2,1,0:T(8,128)(2,1)} %bitcast.3, bf16[]{:T(256)} %constant.4.clone.1), padding=0_0x0_0x0_3 | pad | bytes 400002 | tf_op jit(solution)/shard_map/jit(_pad)/pad | solution.py:235
  2.6 0.0 copy-done
  2.6 0.0 copy-done.1
  2.6 38.2 %shard_map.59 = (bf16[64,8,128]{2,1,0:T(8,128)(2,1)S(1)}, f32[64,8,128]{2,1,0:T(8,128)S(1)}) custom-call(f32[64,8,128]{2,1,0:T(8,128)S(1)} %copy-done, f32[1,128]{1,0:T(1,128)S(1)} %pad_bitcast_fusion.line_ref, f32[25,8,128]{2,1,0:T(8,128)S(1)} %copy-done.1, bf16[25,64,64]{2,1,0:T(8,128)(2,1)S(1)} %pad.9.tmpl_ref), custom_call_target="tpu_custom_call" | custom-call | tf_op jit(solution)/shard_map/pallas_call | solution.py:242
  40.8 0.7 %copy.8 = bf16[64,8,128]{2,1,0:T(8,128)(2,1)} copy(bf16[64,8,128]{2,1,0:T(8,128)(2,1)S(1)} %get-tuple-element.4) | data formatting | bytes 262144
  41.5 0.7 %copy.9 = f32[64,8,128]{2,1,0:T(8,128)} copy(f32[64,8,128]{2,1,0:T(8,128)S(1)} %get-tuple-element.5) | data formatting | bytes 524288
Async XLA Ops:
  0.6 0.7 %copy-start.2 = (f32[61]{0:T(128)S(1)}, f32[61]{0:T(128)}, u32[]{:S(2)}) copy-start(f32[61]{0:T(128)} %param.5) | copy-start | bytes 736
  1.5 1.2 %copy-start = (f32[64,8,128]{2,1,0:T(8,128)S(1)}, f32[64,8,128]{2,1,0:T(8,128)}, u32[]{:S(2)}) copy-start(f32[64,8,128]{2,1,0:T(8,128)} %raw_ref.1) | copy-start | bytes 786436
  1.5 1.2 %copy-start.1 = (f32[25,8,128]{2,1,0:T(8,128)S(1)}, f32[25,8,128]{2,1,0:T(8,128)}, u32[]{:S(2)}) copy-start(f32[25,8,128]{2,1,0:T(8,128)} %coef_in_ref.1) | copy-start | bytes 307204

commit v3 on v2

--- a/solution.py
+++ b/solution.py
@@ -9,59 +9,91 @@
 
 BLOCK = 4
 EDGE = 2
-
-
-def build_band(tmpl_ref, band_ref):
+CHUNK = 16
+PAIRS = 2
+
+
+def build_band(tmpl_ref, early_ref, late_ref):
     spots, count, slot = tmpl_ref.shape
     flat = jnp.concatenate(
         [tmpl_ref[s].astype(jnp.float32) for s in range(spots)]
         + [jnp.zeros((count, slot), jnp.float32)] * (spots % 2),
         axis=1,
     )
+    stacked = jnp.concatenate(
+        [flat] + [pltpu.roll(flat, b, 1) for b in range(1, BLOCK)], axis=0
+    )
+    tall = jnp.transpose(stacked)
+    chunks = [
+        [tall[s * slot + m * CHUNK : s * slot + (m + 1) * CHUNK] for s in range(spots)]
+        for m in range(slot // CHUNK)
+    ]
+    blank = [tall[spots * slot :]] if spots % 2 else []
+    for order, band_ref in ((chunks, early_ref), (chunks[::-1], late_ref)):
+        pieces = [piece for chunk in order for piece in chunk] + blank
+        band_ref[...] = jnp.transpose(jnp.concatenate(pieces, axis=0)).astype(jnp.bfloat16)
+
+
+def build_copies(row, block, copies_ref, start, length):
+    span = block.shape[0]
+    for b in range(5):
+        moved = shift_columns(block, 2 - b)
+        for phase in range(CHUNK // BLOCK):
+            late = moved if phase == 0 else pltpu.roll(moved, span - BLOCK * phase, 0)
+            copies_ref[b, phase, row, start : start + length] = late[:length].astype(jnp.bfloat16)
+
+
+def patch_of(copies_ref, phase, r, group, chunks):
+    return jnp.concatenate(
+        [
+            jnp.concatenate(
+                [
+                    copies_ref[b, phase, r + e + a, (group + m) * CHUNK : (group + m + 1) * CHUNK, :]
+                    for e in range(2)
+                ],
+                axis=1,
+            )
+            for m in chunks
+            for a in range(5)
+            for b in range(5)
+        ],
+        axis=0,
+    )
+
+
+def store_best(scores, t, r, best_ref):
+    count = scores.shape[0] // BLOCK
+    cols = best_ref.shape[2]
     for b in range(BLOCK):
-        moved = flat if b == 0 else pltpu.roll(flat, b, 1)
-        band_ref[b * count : (b + 1) * count, :] = moved.astype(jnp.bfloat16)
-
-
-def build_copies(row, block, copies_ref):
-    span, cols = block.shape
-    lane = lax.broadcasted_iota(jnp.int32, (span, cols), 1)
-    for b in range(5):
-        by = 2 - b
-        moved = block if by == 0 else pltpu.roll(block, by % cols, 1)
-        if by > 0:
-            moved = jnp.where(lane >= by, moved, 0.0)
-        elif by < 0:
-            moved = jnp.where(lane < cols + by, moved, 0.0)
-        for phase in range(4):
-            late = moved if phase == 0 else pltpu.roll(moved, span - 4 * phase, 0)
-            copies_ref[b, phase, row] = late.astype(jnp.bfloat16)
-
-
-def correlate_block(j, copies_ref, band_ref, best_ref, slot):
-    count = band_ref.shape[0] // BLOCK
-    rows = best_ref.shape[1]
-    cols = best_ref.shape[2]
-    depth = 25 * slot
-    phase = lax.rem(j, 4)
-    base = pl.multiple_of((j // 4) * 16, 16)
-    band = band_ref[:, :depth]
-    for r in range(0, rows, 2):
-        patch = jnp.concatenate(
-            [
-                jnp.concatenate(
-                    [copies_ref[b, phase, r + e + a, pl.ds(base, slot), :] for e in range(2)], axis=1
+        top = jnp.max(scores[b * count : (b + 1) * count], axis=0, keepdims=True)
+        for e in range(2):
+            best_ref[t + b, pl.ds(r + e, 1), :] = top[:, e * cols : (e + 1) * cols]
+
+
+def correlate(phase, r, is_first, late, copies_ref, early_ref, late_ref, part_ref, best_ref, groups, total):
+    pair = r // 2
+    for group in range(groups):
+        here = max(0, min(total, groups - group - (0 if is_first else 1)))
+        t = group * CHUNK + phase * BLOCK
+        depth = 25 * CHUNK
+        if not late:
+            if here:
+                patch = patch_of(copies_ref, phase, r, group, range(here))
+                scores = jnp.dot(
+                    early_ref[:, : here * depth], patch, preferred_element_type=jnp.float32
                 )
-                for a in range(5)
-                for b in range(5)
-            ],
-            axis=0,
-        )
-        scores = jnp.dot(band, patch, preferred_element_type=jnp.float32)
-        for b in range(BLOCK):
-            top = jnp.max(scores[b * count : (b + 1) * count], axis=0, keepdims=True)
-            for e in range(2):
-                best_ref[BLOCK * j + b, r + e : r + e + 1, :] = top[:, e * cols : (e + 1) * cols]
+                if here == total:
+                    store_best(scores, t, r, best_ref)
+                else:
+                    part_ref[group, phase, pair] = scores
+        elif here < total:
+            patch = patch_of(copies_ref, phase, r, group, range(total - 1, here - 1, -1))
+            scores = jnp.dot(
+                late_ref[:, : (total - here) * depth], patch, preferred_element_type=jnp.float32
+            )
+            if here:
+                scores = scores + part_ref[group, phase, pair]
+            store_best(scores, t, r, best_ref)
 
 
 def filter_rows(line_ref, ext_ref, filt_ref):
@@ -115,8 +147,8 @@
 def fused_kernel(
     row_parts, time_parts, taps_back,
     raw_ref, line_ref, coef_in_ref, tmpl_ref, white_out_ref, best_ref,
-    ext_ref, coef_ref, filt_ref, moved_ref, white_ref, turned_ref, copies_ref, band_ref,
-    send_sem, recv_sem,
+    ext_ref, coef_ref, filt_ref, moved_ref, white_ref, turned_ref, copies_ref, early_ref, late_ref,
+    part_ref,    send_sem, recv_sem,
 ):
     steps, rows, cols = raw_ref.shape
     slot = tmpl_ref.shape[2]
@@ -192,11 +224,11 @@
     start(coef_down, has_low)
     start(coef_up, has_high)
     ext_ref[steps:] = raw_ref[...]
-    build_band(tmpl_ref, band_ref)
     arrived(raw_copy, has_prev)
     filter_rows(line_ref, ext_ref, filt_ref)
     start(filt_down, has_low)
     start(filt_up, has_high)
+    build_band(tmpl_ref, early_ref, late_ref)
     arrived(coef_down, has_high)
     arrived(coef_up, has_low)
     arrived(filt_down, has_high)
@@ -204,20 +236,43 @@
     whiten_rows(filt_ref, moved_ref, coef_ref, white_ref, turned_ref)
     start(white_copy, has_prev)
     white_out_ref[...] = turned_ref[...].astype(jnp.bfloat16)
+
+    def copies_here(row, carry):
+        build_copies(row, white_ref[0, row].astype(jnp.float32), copies_ref, 0, steps)
+        return carry
+
+    def copies_late(row, carry):
+        block = jnp.concatenate([white_ref[0, row, steps - CHUNK :], white_ref[1, row]], axis=0)
+        build_copies(row, block.astype(jnp.float32), copies_ref, steps - CHUNK, slot)
+        return carry
+
+    phases = CHUNK // BLOCK
+    splits = rows // (2 * PAIRS)
+
+    def run(late):
+        def work(phase, part, is_first):
+            for pair in range(PAIRS):
+                correlate(
+                    phase, part * (2 * PAIRS) + 2 * pair, is_first, late, copies_ref,
+                    early_ref, late_ref, part_ref, best_ref, steps // CHUNK, slot // CHUNK,
+                )
+
+        def first(part, carry):
+            work(0, part, True)
+            return carry
+
+        def others(i, carry):
+            work(1 + i // splits, i % splits, False)
+            return carry
+
+        lax.fori_loop(0, splits, first, 0)
+        lax.fori_loop(0, (phases - 1) * splits, others, 0)
+
+    lax.fori_loop(0, rows + 2 * EDGE, copies_here, 0)
+    run(False)
     arrived(white_copy, has_next)
-
-    def copies(row, carry):
-        block = jnp.concatenate([white_ref[0, row], white_ref[1, row]], axis=0)
-        build_copies(row, block.astype(jnp.float32), copies_ref)
-        return carry
-
-    lax.fori_loop(0, rows + 2 * EDGE, copies, 0)
-
-    def step(j, carry):
-        correlate_block(j, copies_ref, band_ref, best_ref, slot)
-        return carry
-
-    lax.fori_loop(0, steps // BLOCK, step, 0)
+    lax.fori_loop(0, rows + 2 * EDGE, copies_late, 0)
+    run(True)
     sent(raw_copy, has_next)
     sent(coef_down, has_low)
     sent(coef_up, has_high)
@@ -254,8 +309,12 @@
             pltpu.VMEM((5, rows + 4 * EDGE, steps, cols), jnp.float32),
             pltpu.VMEM((2, wide, steps, cols), jnp.bfloat16),
             pltpu.VMEM((steps, rows, cols), jnp.float32),
-            pltpu.VMEM((5, 4, wide, 2 * steps, cols), jnp.bfloat16),
+            pltpu.VMEM((5, CHUNK // BLOCK, wide, steps + slot - CHUNK, cols), jnp.bfloat16),
             pltpu.VMEM((BLOCK * count, (spots + spots % 2) * slot), jnp.bfloat16),
+            pltpu.VMEM((BLOCK * count, (spots + spots % 2) * slot), jnp.bfloat16),
+            pltpu.VMEM(
+                (steps // CHUNK, CHUNK // BLOCK, rows // 2, BLOCK * count, 2 * cols), jnp.float32
+            ),
             pltpu.SemaphoreType.DMA((6,)),
             pltpu.SemaphoreType.DMA((6,)),
         ],

time: 42.4 us -> 38.2 us (0.901)
  the two profiles are of different devices: /device:TPU:1 before, /device:TPU:28 now
where the time goes in v3:
time: 38.2 us; the launch traced here: 38 us
  Pallas kernels  34 us (89%)
  local copies, waits for them, and re-layouts  3.34 us (9%)
  between operations  0.67 us (2%)
    pallas_call x1, Pallas kernels, shards(): pl.pallas_call(kernel, out_shape=(jax.ShapeDtypeStruct((steps, rows, cols...  34 us
    unnamed x8, local copies, waits for them, and re-layouts  2.02 us
    pad x1, local copies, waits for them, and re-layouts, shards(): jnp.pad(jnp.transpose(templates, (2, 0, 1)), ((0, 0), (0, 0), (0, slot -...  1.15 us

profile of v3, /device:TPU:28, one launch (start us, length us, event | category | flops | bytes accessed | tf_op | source)
XLA Modules:
  0.0 38.0 jit_solution(6049027042808936411)
XLA Ops:
  0.6 0.0 copy-start.2
  0.6 0.6 %copy-done.2 = f32[61]{0:T(128)S(1)} copy-done((f32[61]{0:T(128)S(1)}, f32[61]{0:T(128)}, u32[]{:S(2)}) %copy-start.2) | copy-done | bytes 268
  1.3 0.1 rev.3
  1.4 0.1 pad_bitcast_fusion.line_ref
  1.5 0.0 copy-start
  1.5 0.0 copy-start.1
  1.5 1.1 %pad.9.tmpl_ref = bf16[25,64,64]{2,1,0:T(8,128)(2,1)S(1)} pad(bf16[25,64,61]{2,1,0:T(8,128)(2,1)} %bitcast.3, bf16[]{:T(256)} %constant.4.clone.1), padding=0_0x0_0x0_3 | pad | bytes 400002 | tf_op jit(solution)/shard_map/jit(_pad)/pad | solution.py:290
  2.6 0.0 copy-done
  2.6 0.0 copy-done.1
  2.6 34.0 %shard_map.59 = (bf16[64,8,128]{2,1,0:T(8,128)(2,1)S(1)}, f32[64,8,128]{2,1,0:T(8,128)S(1)}) custom-call(f32[64,8,128]{2,1,0:T(8,128)S(1)} %copy-done, f32[1,128]{1,0:T(1,128)S(1)} %pad_bitcast_fusion.line_ref, f32[25,8,128]{2,1,0:T(8,128)S(1)} %copy-done.1, bf16[25,64,64]{2,1,0:T(8,128)(2,1)S(1)} %pad.9.tmpl_ref), custom_call_target="tpu_custom_call" | custom-call | tf_op jit(solution)/shard_map/pallas_call | solution.py:297
  36.7 0.7 %copy.8 = bf16[64,8,128]{2,1,0:T(8,128)(2,1)} copy(bf16[64,8,128]{2,1,0:T(8,128)(2,1)S(1)} %get-tuple-element.4) | data formatting | bytes 262144
  37.3 0.7 %copy.9 = f32[64,8,128]{2,1,0:T(8,128)} copy(f32[64,8,128]{2,1,0:T(8,128)S(1)} %get-tuple-element.5) | data formatting | bytes 524288
Async XLA Ops:
  0.6 0.7 %copy-start.2 = (f32[61]{0:T(128)S(1)}, f32[61]{0:T(128)}, u32[]{:S(2)}) copy-start(f32[61]{0:T(128)} %param.5) | copy-start | bytes 736
  1.5 1.2 %copy-start = (f32[64,8,128]{2,1,0:T(8,128)S(1)}, f32[64,8,128]{2,1,0:T(8,128)}, u32[]{:S(2)}) copy-start(f32[64,8,128]{2,1,0:T(8,128)} %raw_ref.1) | copy-start | bytes 786436
  1.5 1.2 %copy-start.1 = (f32[25,8,128]{2,1,0:T(8,128)S(1)}, f32[25,8,128]{2,1,0:T(8,128)}, u32[]{:S(2)}) copy-start(f32[25,8,128]{2,1,0:T(8,128)} %coef_in_ref.1) | copy-start | bytes 307204
